TPU v7x, 32 devices: a whole 2x2x4 slice. The times are simulated.
32 devices in a mesh: grid: 8 (over z, x), cols: 4 (over y, core).
Axes of the slice: x: 2, y: 2, z: 4, core: 2. Of those that a mesh axis runs over, the one named last changes fastest.
Arguments:
- basis: float32 [1024, 3, 16, 1024], P('cols', None, 'grid'), may hold values from -1 to 1
- snapshots: float32 [128, 3, 16, 1024], P('cols', None, 'grid'), may hold values from -60 to 60
- permittivity: float32 [3, 16, 1024], P(None, 'grid'), may hold values from 1 to 10
- labels: int32 [16, 1024], P('grid'), may hold values from 0 to 7
- sigma_table: float32 [8], replicated, may hold values from 0.1 to 10
Outputs:
- new_basis: float32 [128, 3, 16, 1024], P('cols', None, 'grid')
- coefficients: float32 [1024, 128], P('cols')
- cross_terms: float32 [3, 1024, 128], P(None, 'cols')
- block_terms: float32 [3, 128, 128], P(None, 'cols')
All inputs are finite; a program needn't handle non-finite values.
Results may differ from a plain program's by a relative error of at most 0.0003.
Values sent between devices are 32-bit elements; how exact they have to be, the bound alone decides.
A program may use at most 128 MiB of HBM per device.

v0:
```python
import jax
import jax.numpy as jnp
from jax import lax
from jax.sharding import PartitionSpec as P

NY = 32
HIGHEST = lax.Precision.HIGHEST


def padded(shard, sides, width):
    for axis, dim in sides:
        size, length = (lax.axis_size(axis), shard.shape[dim])
        up = [(i, (i + 1) % size) for i in range(size - 1)]
        down = [(j, i) for i, j in up]
        last = lax.slice_in_dim(shard, length - width, length, axis=dim)
        leading = lax.slice_in_dim(shard, 0, width, axis=dim)
        before = lax.ppermute(last, axis, up)
        after = lax.ppermute(leading, axis, down)
        shard = jnp.concatenate([before, shard, after], axis=dim)
    return shard


def cells_dot(left_rows, right_rows):
    left_flat = left_rows.reshape(left_rows.shape[0], -1)
    right_flat = right_rows.reshape(right_rows.shape[0], -1)
    return lax.dot_general(
        left_flat,
        right_flat,
        (((1,), (1,)), ((), ())),
        precision=HIGHEST,
        preferred_element_type=jnp.float32,
    )


def combine_rows(weights, fields):
    flattened = fields.reshape(fields.shape[0], -1)
    output_rows = lax.dot_general(
        weights,
        flattened,
        (((0,), (0,)), ((), ())),
        precision=HIGHEST,
        preferred_element_type=jnp.float32,
    )
    return output_rows.reshape((weights.shape[1],) + fields.shape[1:])


def forward_x(field, row_len):
    padding_cols = jnp.zeros(field.shape[:-1] + (row_len,), field.dtype)
    return jnp.concatenate([field[..., row_len:], padding_cols], axis=-1)


def backward_x(field, row_len):
    padding_cols = jnp.zeros(field.shape[:-1] + (row_len,), field.dtype)
    return jnp.concatenate([padding_cols, field[..., :-row_len]], axis=-1)


def forward_y(field, row_len):
    column_pos = lax.broadcasted_iota(jnp.int32, (field.shape[-1],), 0) % row_len
    padding_cols = jnp.zeros(field.shape[:-1] + (1,), field.dtype)
    shifted = jnp.concatenate([field[..., 1:], padding_cols], axis=-1)
    return jnp.where(column_pos != row_len - 1, shifted, 0.0)


def backward_y(field, row_len):
    column_pos = lax.broadcasted_iota(jnp.int32, (field.shape[-1],), 0) % row_len
    padding_cols = jnp.zeros(field.shape[:-1] + (1,), field.dtype)
    shifted = jnp.concatenate([padding_cols, field[..., :-1]], axis=-1)
    return jnp.where(column_pos != 0, shifted, 0.0)


def curl_curl(extended, row_len):
    field_x = extended[:, 0]
    field_y = extended[:, 1]
    field_z = extended[:, 2]

    def middle(field):
        return field[:, 1:-1]

    def plus_x(field):
        return forward_x(field, row_len) - field

    def minus_x(field):
        return field - backward_x(field, row_len)

    def plus_y(field):
        return forward_y(field, row_len) - field

    def minus_y(field):
        return field - backward_y(field, row_len)

    def second_x(field):
        return forward_x(field, row_len) - 2.0 * field + backward_x(field, row_len)

    def second_y(field):
        return forward_y(field, row_len) - 2.0 * field + backward_y(field, row_len)

    def second_z(field):
        return field[:, 2:] - 2.0 * field[:, 1:-1] + field[:, :-2]

    curl_x = (
        -second_y(middle(field_x))
        - second_z(field_x)
        + minus_y(plus_x(middle(field_y)))
        + plus_x(middle(field_z))
        - plus_x(field_z[:, :-2])
    )
    curl_y = (
        -second_x(middle(field_y))
        - second_z(field_y)
        + minus_x(plus_y(middle(field_x)))
        + plus_y(middle(field_z))
        - plus_y(field_z[:, :-2])
    )
    curl_z = (
        -second_x(middle(field_z))
        - second_y(middle(field_z))
        + minus_x(field_x[:, 2:] - middle(field_x))
        + minus_y(field_y[:, 2:] - middle(field_y))
    )
    return jnp.stack([curl_x, curl_y, curl_z], axis=1)


def lookup_sigma(labels, sigma_table):
    region_ids = jnp.arange(sigma_table.shape[0], dtype=jnp.int32)
    picked = jnp.where(labels[None] == region_ids[:, None, None], sigma_table[:, None, None], 0.0)
    return jnp.sum(picked, axis=0)


def apply_ops(fields, permittivity, conductivity):
    extended = padded(fields, (("grid", 2),), 1)
    curl_term = curl_curl(extended, NY)
    mass_term = permittivity[None] * fields
    loss_term = conductivity[None, None] * fields
    return (curl_term, mass_term, loss_term)


def shards(basis, snapshots, permittivity, labels, sigma_table):
    basis_cols = basis.shape[0]
    snap_cols = snapshots.shape[0]
    total_snap = snap_cols * lax.axis_size("cols")
    unknowns = 3 * snapshots.shape[3] * snapshots.shape[2] * lax.axis_size("grid")
    conductivity = lookup_sigma(labels, sigma_table)
    current = snapshots
    coefficients = jnp.zeros((basis_cols, total_snap), jnp.float32)
    for sweep_index in range(2):
        partial_value = cells_dot(basis, lax.all_gather(current, "cols", axis=0, tiled=True))
        coef_part = lax.psum(partial_value, "grid")
        current = current - lax.psum_scatter(
            combine_rows(coef_part, basis), "cols", scatter_dimension=0, tiled=True
        )
        coefficients = coefficients + coef_part
    finished = lax.all_gather(current, "cols", axis=0, tiled=True)
    own_start = lax.axis_index("cols") * snap_cols
    identity = jnp.eye(total_snap, dtype=jnp.float32)
    gram_sum = lax.psum(cells_dot(finished, finished) / unknowns, "grid")
    lower_factor = jnp.linalg.cholesky(gram_sum)
    inverse = jax.scipy.linalg.solve_triangular(lower_factor, identity, lower=True)
    new_all = combine_rows(inverse.T, finished)
    curl_term, mass_term, loss_term = apply_ops(new_all, permittivity, conductivity)
    own_new = lax.dynamic_slice_in_dim(new_all, own_start, snap_cols, 0)
    cross_part = jnp.stack(
        [cells_dot(basis, curl_term), cells_dot(basis, mass_term), cells_dot(basis, loss_term)],
        axis=0,
    )
    block_part = (
        jnp.stack(
            [
                cells_dot(own_new, curl_term),
                cells_dot(own_new, mass_term),
                cells_dot(own_new, loss_term),
            ],
            axis=0,
        )
        / unknowns
    )
    cross_terms, block_terms = lax.psum((cross_part, block_part), "grid")
    return (own_new, coefficients, cross_terms, block_terms)


def solution(mesh):
    placed = (
        P("cols", None, "grid", None),
        P("cols", None, "grid", None),
        P(None, "grid", None),
        P("grid", None),
        P(),
    )
    return jax.shard_map(
        shards,
        mesh=mesh,
        in_specs=placed,
        out_specs=(
            P("cols", None, "grid", None),
            P("cols", None),
            P(None, "cols", None),
            P(None, "cols", None),
        ),
        check_vma=False,
    )
```

profile of v0, /device:TPU:0, one launch (start us, length us, event | category | flops | bytes accessed | tf_op | source)
XLA Modules:
  0.0 642.6 jit_solution(8649278137576237144)
XLA Ops:
  9.5 31.9 %all-gather.4.cloned.1.call-done = f32[128,3,2,1024]{3,0,2,1:T(8,128)} async-done(((f32[32,3,2,1024]{3,0,2,1:T(8,128)}), f32[128,3,2,1024]{3,0,2,1:T(8,128)}) %all-gather.4.cloned.1.call-update) | async-done | bytes 3145744 | tf_op jit(solution)/shard_map/all_gather | solution.py:146
  41.4 10.8 %fusion.23 = f32[256,128]{1,0:T(8,128)} fusion(f32[128,3,2,1024]{3,0,2,1:T(8,128)} %all-gather.4.cloned.1.call-done, f32[256,3,2,1024]{3,2,1,0:T(2,128)} %param.5), kind=kOutput, calls=%fused_computation.28 | convolution fusion | flops 2415919104 | bytes 9568256 | tf_op jit(solution)/shard_map/dot_general | solution.py:26
  52.2 9.0 %reshape.49 = f32[256,6144]{1,0:T(8,128)} reshape(f32[256,3,2,1024]{3,2,1,0:T(2,128)} %param.5) | data formatting | bytes 12582912 | tf_op jit(solution)/shard_map/reshape | solution.py:24
  61.2 6.6 %copy.42 = f32[6144,256]{1,0:T(8,128)} copy(f32[6144,256]{0,1:T(8,128)} %bitcast.112) | data formatting | bytes 12582912 | tf_op jit(solution)/shard_map/dot_general | solution.py:37
  67.8 54.2 %all-reduce.19.cloned.1.call-done = f32[256,128]{1,0:T(8,128)} async-done(((f32[256,128]{1,0:T(8,128)}), f32[256,128]{1,0:T(8,128)}) %all-reduce.19.cloned.1.call-update) | async-done | bytes 131088 | tf_op jit(solution)/shard_map/psum | solution.py:147
  122.0 11.2 %fusion.63 = f32[128,3,2,1024]{3,0,2,1:T(8,128)} fusion(f32[3,2,1024,256]{3,2,1,0:T(8,128)} %bitcast.110, f32[256,128]{1,0:T(8,128)} %all-reduce.19.cloned.1.call-done), kind=kOutput, calls=%fused_computation.61 | convolution fusion | flops 2415919104 | bytes 9568256 | tf_op jit(solution)/shard_map/dot_general | solution.py:37
  133.6 37.1 %reduce-scatter.3.cloned.1.call-done = f32[32,3,2,1024]{3,0,2,1:T(8,128)} async-done(((f32[128,3,2,1024]{3,0,2,1:T(8,128)}), f32[32,3,2,1024]{3,0,2,1:T(8,128)}) %reduce-scatter.3.cloned.1.call-update) | async-done | bytes 786448 | tf_op jit(solution)/shard_map/reduce_scatter | solution.py:148
  173.1 28.6 %all-gather.6.cloned.1.call-done = f32[128,3,2,1024]{3,0,2,1:T(8,128)} async-done(((f32[32,3,2,1024]{3,0,2,1:T(8,128)}), f32[128,3,2,1024]{3,0,2,1:T(8,128)}) %all-gather.6.cloned.1.call-update) | async-done | bytes 3145744 | tf_op jit(solution)/shard_map/all_gather | solution.py:146
  201.7 10.7 %fusion.26 = f32[256,128]{1,0:T(8,128)} fusion(f32[128,3,2,1024]{3,0,2,1:T(8,128)} %all-gather.6.cloned.1.call-done, f32[256,3,2,1024]{3,2,1,0:T(2,128)} %param.5), kind=kOutput, calls=%fused_computation.29 | convolution fusion | flops 2415919104 | bytes 9568256 | tf_op jit(solution)/shard_map/dot_general | solution.py:26
  212.4 69.8 %all-reduce.21.cloned.1.call-done = f32[256,128]{1,0:T(8,128)} async-done(((f32[256,128]{1,0:T(8,128)}), f32[256,128]{1,0:T(8,128)}) %all-reduce.21.cloned.1.call-update) | async-done | bytes 131088 | tf_op jit(solution)/shard_map/psum | solution.py:147
  282.2 11.2 %fusion.61 = f32[128,3,2,1024]{3,0,2,1:T(8,128)} fusion(f32[3,2,1024,256]{3,2,1,0:T(8,128)} %bitcast.111, f32[256,128]{1,0:T(8,128)} %all-reduce.21.cloned.1.call-done), kind=kOutput, calls=%fused_computation.59 | convolution fusion | flops 2415919104 | bytes 9568256 | tf_op jit(solution)/shard_map/dot_general | solution.py:37
  293.5 37.3 %reduce-scatter.5.cloned.1.call-done = f32[32,3,2,1024]{3,0,2,1:T(8,128)} async-done(((f32[128,3,2,1024]{3,0,2,1:T(8,128)}), f32[32,3,2,1024]{3,0,2,1:T(8,128)}) %reduce-scatter.5.cloned.1.call-update) | async-done | bytes 786448 | tf_op jit(solution)/shard_map/reduce_scatter | solution.py:148
  333.4 28.2 %all-gather.8.cloned.1.call-done = f32[128,3,2,1024]{3,0,2,1:T(8,128)} async-done(((f32[32,3,2,1024]{3,0,2,1:T(8,128)}), f32[128,3,2,1024]{3,0,2,1:T(8,128)}) %all-gather.8.cloned.1.call-update) | async-done | bytes 3145744 | tf_op jit(solution)/shard_map/all_gather | solution.py:152
  361.7 6.3 fusion.42
  370.4 66.2 %all-reduce.23.cloned.1.call-done = f32[128,128]{0,1:T(8,128)} async-done(((f32[128,128]{0,1:T(8,128)}), f32[128,128]{0,1:T(8,128)}) %all-reduce.23.cloned.1.call-update) | async-done | bytes 65552 | tf_op jit(solution)/shard_map/psum | solution.py:155
  438.4 11.7 %cholesky.17 = f32[128,128]{1,0:T(8,128)S(1)} custom-call(f32[128,128]{1,0:T(8,128)S(1)} %fusion.67), custom_call_target="Cholesky" | custom-call | tf_op jit(solution)/shard_map/jit(cholesky)/cholesky | solution.py:156
  451.4 9.8 %custom-call.7 = f32[1,128,128]{1,2,0:T(8,128)S(1)} custom-call(f32[1,128,128]{2,1,0:T(8,128)S(1)} %fusion.65), custom_call_target="InvertDiagBlocksLowerTriangular" | custom-call | tf_op jit(solution)/shard_map/jit(_solve_triangular)/triangular_solve | solution.py:157
  461.5 4.7 fusion.10
  479.0 9.9 %fusion.37 = f32[1,256,128]{1,2,0:T(8,128)S(1)} fusion(f32[256,3,2,1024]{3,2,1,0:T(2,128)} %param.5, f32[128,3,2,1024]{3,0,2,1:T(8,128)S(1)} %fusion.10, f32[2,1024]{1,0:T(2,128)S(1)} %select_reduce_fusion), kind=kOutput, calls=%fused_computation.32 | convolution fusion | flops 2416705536 | bytes 9576448 | tf_op jit(solution)/shard_map/dot_general | solution.py:26
  488.9 7.2 %fusion.32 = f32[1,256,128]{1,2,0:T(8,128)S(1)} fusion(f32[256,3,2,1024]{3,2,1,0:T(2,128)S(1)} %bitcast.109, f32[128,3,2,1024]{3,0,2,1:T(8,128)S(1)} %fusion.10, f32[3,2,1024]{2,1,0:T(2,128)S(1)} %copy-done.15), kind=kOutput, calls=%fused_computation.31 | convolution fusion | flops 2416705536 | bytes 9592832 | tf_op jit(solution)/shard_map/dot_general | solution.py:26
  496.2 41.0 %collective-permute-done = f32[128,3,1,1024]{3,0,2,1:T(8,128)} collective-permute-done((f32[128,3,1,1024]{3,0,2,1:T(8,128)}, f32[128,3,1,1024]{3,0,2,1:T(8,128)}, u32[]{:S(2)}, u32[]{:S(2)}) %collective-permute-start) | collective-permute-done | bytes 1572896 | tf_op jit(solution)/shard_map/ppermute | solution.py:17
  553.0 7.3 %fusion.29 = f32[1,256,128]{1,2,0:T(8,128)S(1)} fusion(f32[256,3,2,1024]{3,2,1,0:T(2,128)S(1)} %bitcast.109, f32[128,1,2,1024]{3,0,2,1:T(8,128)S(1)} %add_bitcast_fusion, f32[128,1,2,1024]{3,0,2,1:T(8,128)S(1)} %fusion.54, f32[128,1,2,1024]{3,0,2,1:T(8,128)S(1)} %get-tuple-element.19), kind=kOutput, calls=%fused_computation.30 | convolution fusion | flops 2417491968 | bytes 9568256 | tf_op jit(solution)/shard_map/dot_general | solution.py:26
  570.3 37.2 %psum.39 = f32[3,32,128]{2,1,0:T(8,128)} all-reduce(f32[3,32,128]{2,1,0:T(8,128)S(1)} %maximum_multiply_fusion), channel_id=1, replica_groups=mesh['grid'=8,'cols'=4] {'grid'}, use_global_device_ids=true, to_apply=%region_9.10 | all-reduce | flops 12288 | bytes 98304 | tf_op jit(solution)/shard_map/psum | solution.py:176
  607.5 26.2 %all-reduce.25.cloned.1.call-done = f32[3,256,128]{1,2,0:T(8,128)} async-done(((f32[3,256,128]{1,2,0:T(8,128)}), f32[3,256,128]{1,2,0:T(8,128)}) %all-reduce.25.cloned.1.call-update) | async-done | bytes 393232 | tf_op jit(solution)/shard_map/psum | solution.py:176
  (92 shorter events, 53.7 us)
Async XLA Ops:
  7.2 34.2 %all-gather.4.cloned.1.call-start = ((), (), s32[]{:S(2)}) async-start(), calls=%async_computation.2 | async-start | bytes 3932160 | tf_op jit(solution)/shard_map/all_gather | solution.py:146
  9.5 112.6 %all-reduce.19.cloned.1.call-start = ((), (), s32[]{:S(2)}) async-start(), calls=%async_computation.3 | async-start | bytes 262144 | tf_op jit(solution)/shard_map/psum | solution.py:147
  52.2 118.5 %reduce-scatter.3.cloned.1.call-start = ((), (), s32[]{:S(2)}) async-start(), calls=%async_computation.4 | async-start | bytes 3932160 | tf_op jit(solution)/shard_map/reduce_scatter | solution.py:148
  133.3 37.4 %copy-start.12 = (f32[32,3,2,1024]{3,2,1,0:T(2,128)S(1)}, f32[32,3,2,1024]{3,2,1,0:T(2,128)}, u32[]{:S(2)}) copy-start(f32[32,3,2,1024]{3,2,1,0:T(2,128)} %param.6) | copy-start | bytes 2359300
  133.3 68.4 %all-gather.6.cloned.1.call-start = ((), (), s32[]{:S(2)}) async-start(), calls=%async_computation.5 | async-start | bytes 3932160 | tf_op jit(solution)/shard_map/all_gather | solution.py:146
  173.0 109.2 %all-reduce.21.cloned.1.call-start = ((), (), s32[]{:S(2)}) async-start(), calls=%async_computation.6 | async-start | bytes 262144 | tf_op jit(solution)/shard_map/psum | solution.py:147
  212.4 118.5 %reduce-scatter.5.cloned.1.call-start = ((), (), s32[]{:S(2)}) async-start(), calls=%async_computation.7 | async-start | bytes 3932160 | tf_op jit(solution)/shard_map/reduce_scatter | solution.py:148
  293.5 37.4 %copy-start.3 = (f32[32,3,2,1024]{3,0,2,1:T(8,128)S(1)}, f32[32,3,2,1024]{3,0,2,1:T(8,128)}, u32[]{:S(2)}) copy-start(f32[32,3,2,1024]{3,0,2,1:T(8,128)} %copy_subtract_fusion) | copy-start | bytes 2359300
  293.5 68.2 %all-gather.8.cloned.1.call-start = ((), (), s32[]{:S(2)}) async-start(), calls=%async_computation.8 | async-start | bytes 3932160 | tf_op jit(solution)/shard_map/all_gather | solution.py:152
  333.0 103.6 %all-reduce.23.cloned.1.call-start = ((), (), s32[]{:S(2)}) async-start(), calls=%async_computation.9 | async-start | bytes 131072 | tf_op jit(solution)/shard_map/psum | solution.py:155
  361.7 6.4 copy-start
  368.0 265.7 %all-reduce.25.cloned.1.call-start = ((), (), s32[]{:S(2)}) async-start(), calls=%async_computation.10 | async-start | bytes 786432 | tf_op jit(solution)/shard_map/psum | solution.py:176
  466.2 7.9 %copy-start.16 = (s32[2,1024]{1,0:T(2,128)S(1)}, s32[2,1024]{1,0:T(2,128)}, u32[]{:S(2)}) copy-start(s32[2,1024]{1,0:T(2,128)} %param.8) | copy-start | bytes 24580
  466.2 7.9 %copy-start.17 = (f32[8]{0:T(128)S(1)}, f32[8]{0:T(128)}, u32[]{:S(2)}) copy-start(f32[8]{0:T(128)} %param.9) | copy-start | bytes 100
  466.2 8.0 %copy-start.13 = (f32[256,128]{1,0:T(8,128)S(1)}, f32[256,128]{1,0:T(8,128)}, u32[]{:S(2)}) copy-start(f32[256,128]{1,0:T(8,128)} %all-reduce.19.cloned.1.call-done) | copy-start | bytes 393220
  466.2 8.0 %copy-start.14 = (f32[256,128]{1,0:T(8,128)S(1)}, f32[256,128]{1,0:T(8,128)}, u32[]{:S(2)}) copy-start(f32[256,128]{1,0:T(8,128)} %all-reduce.21.cloned.1.call-done) | copy-start | bytes 393220
  466.2 9.6 %copy-start.15 = (f32[3,2,1024]{2,1,0:T(2,128)S(1)}, f32[3,2,1024]{2,1,0:T(2,128)}, u32[]{:S(2)}) copy-start(f32[3,2,1024]{2,1,0:T(2,128)} %param.7) | copy-start | bytes 73732
  468.1 69.1 %collective-permute-start = (f32[128,3,1,1024]{3,0,2,1:T(8,128)}, f32[128,3,1,1024]{3,0,2,1:T(8,128)}, u32[]{:S(2)}, u32[]{:S(2)}) collective-permute-start(f32[128,3,1,1024]{3,0,2,1:T(8,128)} %get-tuple-element.21), channel_id=1, source_target_pairs={{0,4},{4,8},{8,12},{12,16},{16,20},{20,24},{24,28},{1,5},{5,9},{9,... | collective-permute-start | bytes 4718600 | tf_op jit(solution)/shard_map/ppermute | solution.py:17
  472.6 64.6 %collective-permute-start.1 = (f32[128,3,1,1024]{3,0,2,1:T(8,128)}, f32[128,3,1,1024]{3,0,2,1:T(8,128)}, u32[]{:S(2)}, u32[]{:S(2)}) collective-permute-start(f32[128,3,1,1024]{3,0,2,1:T(8,128)} %get-tuple-element.22), channel_id=1, source_target_pairs={{4,0},{8,4},{12,8},{16,12},{20,16},{24,20},{28,24},{5,1},{9,5},{13... | collective-permute-start | bytes 4718600 | tf_op jit(solution)/shard_map/ppermute | solution.py:18
  475.8 13.0 %slice-start = ((s8[6291456]{0:T(1024)(128)(4,1)}), s8[4194304]{0:T(1024)(128)(4,1)S(1)}, s32[]{:S(2)}) async-start(s8[6291456]{0:T(1024)(128)(4,1)} %bitcast.108), calls=%async_computation.11 | async-start | bytes 8388608
  479.0 9.9 %slice-start.1 = ((s8[6291456]{0:T(1024)(128)(4,1)}), s8[2097152]{0:T(1024)(128)(4,1)S(1)}, s32[]{:S(2)}) async-start(s8[6291456]{0:T(1024)(128)(4,1)} %bitcast.108), calls=%async_computation.12 | async-start | bytes 4194304
  553.0 7.3 %copy-start.9 = (f32[128,1,2,1024]{3,0,2,1:T(8,128)}, f32[128,1,2,1024]{3,0,2,1:T(8,128)S(1)}, u32[]{:S(2)}) copy-start(f32[128,1,2,1024]{3,0,2,1:T(8,128)S(1)} %add_bitcast_fusion) | copy-start | bytes 3145732
  561.1 6.0 copy-start.5
  561.1 6.0 copy-start.7
  (7 other events, 19.8 us)
Sparse Core Ops, SparseCore 0:
  10.1 31.2 all-gather.3
  52.3 69.6 all-reduce.18
  133.4 37.2 reduce-scatter.2
  173.1 28.5 all-gather.5
  212.5 69.6 all-reduce.20
  293.6 37.2 reduce-scatter.4
  333.1 28.5 all-gather.7
  368.1 68.4 all-reduce.22
  561.2 72.4 all-reduce.24
where the time goes:
time: 652 us; the launch traced here: 643 us
  waiting for transfers between devices  421 us (65%)
  matrix products  90.2 us (14%)
  other arithmetic  38.7 us (6%)
  blocking collectives  37.2 us (6%)
  local copies, waits for them, and re-layouts  34 us (5%)
  between operations  14.7 us (2%)
  starting transfers between devices  6.98 us (1%)
    psum x2, waiting for transfers between devices, shards(): coef_part = lax.psum(partial_value, 'grid')  124 us
    reduce_scatter x2, waiting for transfers between devices, shards(): lax.psum_scatter(combine_rows(coef_part, basis), 'cols', scatter_dimensio...  74.4 us
    psum x1, waiting for transfers between devices, shards(): gram_sum = lax.psum(cells_dot(finished, finished) / unknowns, 'grid')  66.2 us
    dot_general x9, matrix products, cells_dot(): lax.dot_general(left_flat, right_flat, (((1,), (1,)), ((), ())), precisio...  62.8 us
    all_gather x2, waiting for transfers between devices, shards(): lax.all_gather(current, 'cols', axis=0, tiled=True)  60.5 us
    ppermute x1, waiting for transfers between devices, padded(): before = lax.ppermute(last, axis, up)  41 us
    psum x1, blocking collectives, shards(): cross_terms, block_terms = lax.psum((cross_part, block_part), 'grid')  37.2 us
    all_gather x1, waiting for transfers between devices, shards(): finished = lax.all_gather(current, 'cols', axis=0, tiled=True)  28.2 us
  transfers between devices with their start and end apart: 11, of which 10 were waited for; matrix products, arithmetic and copies ran while one was open for 7% of the time, Pallas kernels for 0%

commit v1 on v0

--- a/solution.py
+++ b/solution.py
@@ -144,7 +144,10 @@
     coefficients = jnp.zeros((basis_cols, total_snap), jnp.float32)
     for sweep_index in range(2):
         partial_value = cells_dot(basis, lax.all_gather(current, "cols", axis=0, tiled=True))
-        coef_part = lax.psum(partial_value, "grid")
+        peers, coef_part = (lax.axis_size("grid"), partial_value)
+        for far in [1 << k for k in range(peers.bit_length() - 1)]:
+            swap = [(i_2, i_2 ^ far) for i_2 in range(peers)]
+            coef_part = coef_part + lax.ppermute(coef_part, "grid", swap)
         current = current - lax.psum_scatter(
             combine_rows(coef_part, basis), "cols", scatter_dimension=0, tiled=True
         )

time: 652 us -> 558 us (0.86)
  waiting for transfers between devices: 421 us -> 315 us
  starting transfers between devices: 6.98 us -> 18 us
    psum x2 -> x0, waiting for transfers between devices: 124 us -> none  [shards(): coef_part = lax.psum(partial_value, 'grid')]
    ppermute x0 -> x6, waiting for transfers between devices: none -> 20.3 us  [shards(): coef_part = coef_part + lax.ppermute(coef_part, 'grid', swap)]
    ppermute x0 -> x6, starting transfers between devices: none -> 11.1 us  [shards(): coef_part = coef_part + lax.ppermute(coef_part, 'grid', swap)]
  transfers between devices with their start and end apart: 11 -> 15, of which waited for: 10 -> 13; matrix products, arithmetic and copies ran while one was open for 7% -> 9% of each run, Pallas kernels for 0% -> 0%
where the time goes in v1:
time: 558 us; the launch traced here: 548 us
  waiting for transfers between devices  315 us (56%)
  matrix products  89.6 us (16%)
  other arithmetic  39.5 us (7%)
  blocking collectives  37.2 us (7%)
  local copies, waits for them, and re-layouts  34 us (6%)
  starting transfers between devices  18 us (3%)
  between operations  15 us (3%)
    reduce_scatter x2, waiting for transfers between devices, shards(): lax.psum_scatter(combine_rows(coef_part, basis), 'cols', scatter_dimensio...  74.2 us
    psum x1, waiting for transfers between devices, shards(): gram_sum = lax.psum(cells_dot(finished, finished) / unknowns, 'grid')  65 us
    dot_general x9, matrix products, cells_dot(): lax.dot_general(left_flat, right_flat, (((1,), (1,)), ((), ())), precisio...  62.5 us
    all_gather x2, waiting for transfers between devices, shards(): lax.all_gather(current, 'cols', axis=0, tiled=True)  60.3 us
    ppermute x1, waiting for transfers between devices, padded(): before = lax.ppermute(last, axis, up)  40.3 us
    psum x1, blocking collectives, shards(): cross_terms, block_terms = lax.psum((cross_part, block_part), 'grid')  37.2 us
    all_gather x1, waiting for transfers between devices, shards(): finished = lax.all_gather(current, 'cols', axis=0, tiled=True)  28.6 us
    dot_general x3, matrix products, combine_rows(): lax.dot_general(weights, flattened, (((0,), (0,)), ((), ())), precision=H...  26.9 us
  transfers between devices with their start and end apart: 15, of which 13 were waited for; matrix products, arithmetic and copies ran while one was open for 9% of the time, Pallas kernels for 0%

profile of v1, /device:TPU:0, one launch (start us, length us, event | category | flops | bytes accessed | tf_op | source)
XLA Modules:
  0.0 548.3 jit_solution(4930944442206233257)
XLA Ops:
  9.5 31.9 %all-gather.4.cloned.1.call-done = f32[128,3,2,1024]{3,0,2,1:T(8,128)} async-done(((f32[32,3,2,1024]{3,0,2,1:T(8,128)}), f32[128,3,2,1024]{3,0,2,1:T(8,128)}) %all-gather.4.cloned.1.call-update) | async-done | bytes 3145744 | tf_op jit(solution)/shard_map/all_gather | solution.py:146
  41.4 10.2 %fusion.23 = f32[256,128]{1,0:T(8,128)S(1)} fusion(f32[128,3,2,1024]{3,0,2,1:T(8,128)} %all-gather.4.cloned.1.call-done, f32[256,3,2,1024]{3,2,1,0:T(2,128)} %param.5), kind=kOutput, calls=%fused_computation.28 | convolution fusion | flops 2415919104 | bytes 9568256 | tf_op jit(solution)/shard_map/dot_general | solution.py:26
  64.8 9.0 %reshape.49 = f32[256,6144]{1,0:T(8,128)} reshape(f32[256,3,2,1024]{3,2,1,0:T(2,128)} %param.5) | data formatting | bytes 12582912 | tf_op jit(solution)/shard_map/reshape | solution.py:24
  73.8 6.6 %copy.42 = f32[6144,256]{1,0:T(8,128)} copy(f32[6144,256]{0,1:T(8,128)} %bitcast.112) | data formatting | bytes 12582912 | tf_op jit(solution)/shard_map/dot_general | solution.py:37
  80.4 11.1 %fusion.63 = f32[128,3,2,1024]{3,0,2,1:T(8,128)} fusion(f32[3,2,1024,256]{3,2,1,0:T(8,128)} %bitcast.110, f32[256,128]{1,0:T(8,128)S(1)} %add.146), kind=kOutput, calls=%fused_computation.61 | convolution fusion | flops 2415919104 | bytes 9568256 | tf_op jit(solution)/shard_map/dot_general | solution.py:37
  91.6 36.2 %reduce-scatter.3.cloned.1.call-done = f32[32,3,2,1024]{3,0,2,1:T(8,128)} async-done(((f32[128,3,2,1024]{3,0,2,1:T(8,128)}), f32[32,3,2,1024]{3,0,2,1:T(8,128)}) %reduce-scatter.3.cloned.1.call-update) | async-done | bytes 786448 | tf_op jit(solution)/shard_map/reduce_scatter | solution.py:151
  130.4 28.4 %all-gather.6.cloned.1.call-done = f32[128,3,2,1024]{3,0,2,1:T(8,128)} async-done(((f32[32,3,2,1024]{3,0,2,1:T(8,128)}), f32[128,3,2,1024]{3,0,2,1:T(8,128)}) %all-gather.6.cloned.1.call-update) | async-done | bytes 3145744 | tf_op jit(solution)/shard_map/all_gather | solution.py:146
  158.8 10.1 %fusion.26 = f32[256,128]{1,0:T(8,128)S(1)} fusion(f32[128,3,2,1024]{3,0,2,1:T(8,128)} %all-gather.6.cloned.1.call-done, f32[256,3,2,1024]{3,2,1,0:T(2,128)} %param.5), kind=kOutput, calls=%fused_computation.29 | convolution fusion | flops 2415919104 | bytes 9568256 | tf_op jit(solution)/shard_map/dot_general | solution.py:26
  182.1 5.0 collective-permute-done.5
  187.1 11.1 %fusion.61 = f32[128,3,2,1024]{3,0,2,1:T(8,128)} fusion(f32[3,2,1024,256]{3,2,1,0:T(8,128)} %bitcast.111, f32[256,128]{1,0:T(8,128)S(1)} %add.148, f32[256,128]{1,0:T(8,128)S(1)} %collective-permute-done.5), kind=kOutput, calls=%fused_computation.59 | convolution fusion | flops 2415951872 | bytes 9699328 | tf_op jit(solution)/shard_map/dot_general | solution.py:37
  198.3 38.0 %reduce-scatter.5.cloned.1.call-done = f32[32,3,2,1024]{3,0,2,1:T(8,128)} async-done(((f32[128,3,2,1024]{3,0,2,1:T(8,128)}), f32[32,3,2,1024]{3,0,2,1:T(8,128)}) %reduce-scatter.5.cloned.1.call-update) | async-done | bytes 786448 | tf_op jit(solution)/shard_map/reduce_scatter | solution.py:151
  238.5 28.6 %all-gather.8.cloned.1.call-done = f32[128,3,2,1024]{3,0,2,1:T(8,128)} async-done(((f32[32,3,2,1024]{3,0,2,1:T(8,128)}), f32[128,3,2,1024]{3,0,2,1:T(8,128)}) %all-gather.8.cloned.1.call-update) | async-done | bytes 3145744 | tf_op jit(solution)/shard_map/all_gather | solution.py:155
  267.1 6.3 %fusion.42 = f32[128,128]{0,1:T(8,128)} fusion(f32[128,3,2,1024]{3,0,2,1:T(8,128)} %all-gather.8.cloned.1.call-done), kind=kOutput, calls=%fused_computation.35 | convolution fusion | flops 1207975936 | bytes 3211264 | tf_op jit(solution)/shard_map/dot_general | solution.py:26
  277.0 65.0 %all-reduce.17.cloned.1.call-done = f32[128,128]{0,1:T(8,128)} async-done(((f32[128,128]{0,1:T(8,128)}), f32[128,128]{0,1:T(8,128)}) %all-reduce.17.cloned.1.call-update) | async-done | bytes 65552 | tf_op jit(solution)/shard_map/psum | solution.py:158
  343.8 11.7 %cholesky.17 = f32[128,128]{1,0:T(8,128)S(1)} custom-call(f32[128,128]{1,0:T(8,128)S(1)} %fusion.67), custom_call_target="Cholesky" | custom-call | tf_op jit(solution)/shard_map/jit(cholesky)/cholesky | solution.py:159
  356.9 9.8 %custom-call.7 = f32[1,128,128]{1,2,0:T(8,128)S(1)} custom-call(f32[1,128,128]{2,1,0:T(8,128)S(1)} %fusion.65), custom_call_target="InvertDiagBlocksLowerTriangular" | custom-call | tf_op jit(solution)/shard_map/jit(_solve_triangular)/triangular_solve | solution.py:160
  367.0 4.7 fusion.10
  373.5 4.5 collective-permute-start.6
  385.2 9.9 %fusion.37 = f32[1,256,128]{1,2,0:T(8,128)S(1)} fusion(f32[256,3,2,1024]{3,2,1,0:T(2,128)} %param.5, f32[128,3,2,1024]{3,0,2,1:T(8,128)S(1)} %fusion.10, f32[2,1024]{1,0:T(2,128)S(1)} %select_reduce_fusion), kind=kOutput, calls=%fused_computation.32 | convolution fusion | flops 2416705536 | bytes 9576448 | tf_op jit(solution)/shard_map/dot_general | solution.py:26
  395.1 7.2 %fusion.32 = f32[1,256,128]{1,2,0:T(8,128)S(1)} fusion(f32[256,3,2,1024]{3,2,1,0:T(2,128)S(1)} %bitcast.109, f32[128,3,2,1024]{3,0,2,1:T(8,128)S(1)} %fusion.10, f32[3,2,1024]{2,1,0:T(2,128)S(1)} %copy-done.13), kind=kOutput, calls=%fused_computation.31 | convolution fusion | flops 2416705536 | bytes 9592832 | tf_op jit(solution)/shard_map/dot_general | solution.py:26
  402.4 40.3 %collective-permute-done.6 = f32[128,3,1,1024]{3,0,2,1:T(8,128)} collective-permute-done((f32[128,3,1,1024]{3,0,2,1:T(8,128)}, f32[128,3,1,1024]{3,0,2,1:T(8,128)}, u32[]{:S(2)}, u32[]{:S(2)}) %collective-permute-start.6) | collective-permute-done | bytes 1572896 | tf_op jit(solution)/shard_map/ppermute | solution.py:17
  458.4 7.3 %fusion.29 = f32[1,256,128]{1,2,0:T(8,128)S(1)} fusion(f32[256,3,2,1024]{3,2,1,0:T(2,128)S(1)} %bitcast.109, f32[128,1,2,1024]{3,0,2,1:T(8,128)S(1)} %add_bitcast_fusion, f32[128,1,2,1024]{3,0,2,1:T(8,128)S(1)} %fusion.54, f32[128,1,2,1024]{3,0,2,1:T(8,128)S(1)} %get-tuple-element.19), kind=kOutput, calls=%fused_computation.30 | convolution fusion | flops 2417491968 | bytes 9568256 | tf_op jit(solution)/shard_map/dot_general | solution.py:26
  475.6 37.2 %psum.23 = f32[3,32,128]{2,1,0:T(8,128)} all-reduce(f32[3,32,128]{2,1,0:T(8,128)S(1)} %maximum_multiply_fusion), channel_id=1, replica_groups=mesh['grid'=8,'cols'=4] {'grid'}, use_global_device_ids=true, to_apply=%region_7.8 | all-reduce | flops 12288 | bytes 98304 | tf_op jit(solution)/shard_map/psum | solution.py:179
  512.9 26.2 %all-reduce.19.cloned.1.call-done = f32[3,256,128]{1,2,0:T(8,128)} async-done(((f32[3,256,128]{1,2,0:T(8,128)}), f32[3,256,128]{1,2,0:T(8,128)}) %all-reduce.19.cloned.1.call-update) | async-done | bytes 393232 | tf_op jit(solution)/shard_map/psum | solution.py:179
  (97 shorter events, 77.1 us)
Async XLA Ops:
  7.2 34.2 %all-gather.4.cloned.1.call-start = ((), (), s32[]{:S(2)}) async-start(), calls=%async_computation.2 | async-start | bytes 3932160 | tf_op jit(solution)/shard_map/all_gather | solution.py:146
  9.5 118.3 %reduce-scatter.3.cloned.1.call-start = ((), (), s32[]{:S(2)}) async-start(), calls=%async_computation.3 | async-start | bytes 3932160 | tf_op jit(solution)/shard_map/reduce_scatter | solution.py:151
  51.6 5.7 %collective-permute-start = (f32[256,128]{1,0:T(8,128)S(1)}, f32[256,128]{1,0:T(8,128)S(1)}, u32[]{:S(2)}, u32[]{:S(2)}) collective-permute-start(f32[256,128]{1,0:T(8,128)S(1)} %fusion.23), channel_id=1, source_target_pairs={{0,4},{4,0},{8,12},{12,8},{16,20},{20,16},{24,28},{28,24},{1,5},{5... | collective-permute-start | bytes 393224 | tf_op jit(solution)/shard_map/ppermute | solution.py:150
  57.3 5.0 collective-permute-start.1
  62.3 18.0 %collective-permute-start.2 = (f32[256,128]{1,0:T(8,128)S(1)}, f32[256,128]{1,0:T(8,128)S(1)}, u32[]{:S(2)}, u32[]{:S(2)}) collective-permute-start(f32[256,128]{1,0:T(8,128)S(1)} %add.145), channel_id=1, source_target_pairs={{0,16},{4,20},{8,24},{12,28},{16,0},{20,4},{24,8},{28,12},{1,17},{... | collective-permute-start | bytes 393224 | tf_op jit(solution)/shard_map/ppermute | solution.py:150
  91.5 36.3 %copy-start.12 = (f32[32,3,2,1024]{3,2,1,0:T(2,128)S(1)}, f32[32,3,2,1024]{3,2,1,0:T(2,128)}, u32[]{:S(2)}) copy-start(f32[32,3,2,1024]{3,2,1,0:T(2,128)} %param.6) | copy-start | bytes 2359300
  91.6 67.3 %all-gather.6.cloned.1.call-start = ((), (), s32[]{:S(2)}) async-start(), calls=%async_computation.4 | async-start | bytes 3932160 | tf_op jit(solution)/shard_map/all_gather | solution.py:146
  130.2 106.2 %reduce-scatter.5.cloned.1.call-start = ((), (), s32[]{:S(2)}) async-start(), calls=%async_computation.5 | async-start | bytes 3932160 | tf_op jit(solution)/shard_map/reduce_scatter | solution.py:151
  168.9 5.7 %collective-permute-start.3 = (f32[256,128]{1,0:T(8,128)S(1)}, f32[256,128]{1,0:T(8,128)S(1)}, u32[]{:S(2)}, u32[]{:S(2)}) collective-permute-start(f32[256,128]{1,0:T(8,128)S(1)} %fusion.26), channel_id=1, source_target_pairs={{0,4},{4,0},{8,12},{12,8},{16,20},{20,16},{24,28},{28,24},{1,5},{5... | collective-permute-start | bytes 393224 | tf_op jit(solution)/shard_map/ppermute | solution.py:150
  174.6 5.0 collective-permute-start.4
  179.7 7.5 %collective-permute-start.5 = (f32[256,128]{1,0:T(8,128)S(1)}, f32[256,128]{1,0:T(8,128)S(1)}, u32[]{:S(2)}, u32[]{:S(2)}) collective-permute-start(f32[256,128]{1,0:T(8,128)S(1)} %add.148), channel_id=1, source_target_pairs={{0,16},{4,20},{8,24},{12,28},{16,0},{20,4},{24,8},{28,12},{1,17},{... | collective-permute-start | bytes 393224 | tf_op jit(solution)/shard_map/ppermute | solution.py:150
  198.2 38.1 %copy-start.3 = (f32[32,3,2,1024]{3,0,2,1:T(8,128)S(1)}, f32[32,3,2,1024]{3,0,2,1:T(8,128)}, u32[]{:S(2)}) copy-start(f32[32,3,2,1024]{3,0,2,1:T(8,128)} %copy_subtract_fusion) | copy-start | bytes 2359300
  198.3 68.9 %all-gather.8.cloned.1.call-start = ((), (), s32[]{:S(2)}) async-start(), calls=%async_computation.6 | async-start | bytes 3932160 | tf_op jit(solution)/shard_map/all_gather | solution.py:155
  238.4 35.5 %copy-start.14 = (s32[2,1024]{1,0:T(2,128)S(1)}, s32[2,1024]{1,0:T(2,128)}, u32[]{:S(2)}) copy-start(s32[2,1024]{1,0:T(2,128)} %param.8) | copy-start | bytes 24580
  238.5 103.6 %all-reduce.17.cloned.1.call-start = ((), (), s32[]{:S(2)}) async-start(), calls=%async_computation.7 | async-start | bytes 131072 | tf_op jit(solution)/shard_map/psum | solution.py:158
  267.1 7.5 %copy-start = (f32[128,3,2,1024]{3,0,2,1:T(8,128)S(1)}, f32[128,3,2,1024]{3,0,2,1:T(8,128)}, u32[]{:S(2)}) copy-start(f32[128,3,2,1024]{3,0,2,1:T(8,128)} %all-gather.8.cloned.1.call-done) | copy-start | bytes 9437188
  273.4 265.7 %all-reduce.19.cloned.1.call-start = ((), (), s32[]{:S(2)}) async-start(), calls=%async_computation.8 | async-start | bytes 786432 | tf_op jit(solution)/shard_map/psum | solution.py:179
  373.5 69.1 %collective-permute-start.6 = (f32[128,3,1,1024]{3,0,2,1:T(8,128)}, f32[128,3,1,1024]{3,0,2,1:T(8,128)}, u32[]{:S(2)}, u32[]{:S(2)}) collective-permute-start(f32[128,3,1,1024]{3,0,2,1:T(8,128)} %get-tuple-element.21), channel_id=1, source_target_pairs={{0,4},{4,8},{8,12},{12,16},{16,20},{20,24},{24,28},{1,5},{5,9},{9,... | collective-permute-start | bytes 4718600 | tf_op jit(solution)/shard_map/ppermute | solution.py:17
  378.0 64.6 %collective-permute-start.7 = (f32[128,3,1,1024]{3,0,2,1:T(8,128)}, f32[128,3,1,1024]{3,0,2,1:T(8,128)}, u32[]{:S(2)}, u32[]{:S(2)}) collective-permute-start(f32[128,3,1,1024]{3,0,2,1:T(8,128)} %get-tuple-element.22), channel_id=1, source_target_pairs={{4,0},{8,4},{12,8},{16,12},{20,16},{24,20},{28,24},{5,1},{9,5},{13... | collective-permute-start | bytes 4718600 | tf_op jit(solution)/shard_map/ppermute | solution.py:18
  381.1 13.9 %slice-start = ((s8[6291456]{0:T(1024)(128)(4,1)}), s8[4194304]{0:T(1024)(128)(4,1)S(1)}, s32[]{:S(2)}) async-start(s8[6291456]{0:T(1024)(128)(4,1)} %bitcast.108), calls=%async_computation.9 | async-start | bytes 8388608
  385.2 9.9 %slice-start.1 = ((s8[6291456]{0:T(1024)(128)(4,1)}), s8[2097152]{0:T(1024)(128)(4,1)S(1)}, s32[]{:S(2)}) async-start(s8[6291456]{0:T(1024)(128)(4,1)} %bitcast.108), calls=%async_computation.10 | async-start | bytes 4194304
  385.2 9.9 %copy-start.13 = (f32[3,2,1024]{2,1,0:T(2,128)S(1)}, f32[3,2,1024]{2,1,0:T(2,128)}, u32[]{:S(2)}) copy-start(f32[3,2,1024]{2,1,0:T(2,128)} %param.7) | copy-start | bytes 73732
  458.4 7.3 %copy-start.9 = (f32[128,1,2,1024]{3,0,2,1:T(8,128)}, f32[128,1,2,1024]{3,0,2,1:T(8,128)S(1)}, u32[]{:S(2)}) copy-start(f32[128,1,2,1024]{3,0,2,1:T(8,128)S(1)} %add_bitcast_fusion) | copy-start | bytes 3145732
  466.5 6.0 %copy-start.5 = (f32[128,1,2,1024]{3,0,2,1:T(8,128)S(1)}, f32[128,1,2,1024]{3,0,2,1:T(8,128)}, u32[]{:S(2)}) copy-start(f32[128,1,2,1024]{3,0,2,1:T(8,128)} %copy-done.4) | copy-start | bytes 3145732
  (8 other events, 25.7 us)
Sparse Core Ops, SparseCore 0:
  10.1 31.2 all-gather.3
  91.7 36.0 reduce-scatter.2
  130.3 28.5 all-gather.5
  198.4 37.8 reduce-scatter.4
  238.6 28.5 all-gather.7
  273.6 68.4 all-reduce.16
  466.6 72.4 all-reduce.18
